TPU v7x, 512 devices: a whole 4x4x16 slice. The times are simulated.
512 devices in a mesh: replica: 8 (over z_lo, core), fsdp: 64 (over z_hi, y, x).
Axes of the slice: x: 4, y: 4, z: 16 (z_hi: 4, z_lo: 4; z = z_hi * 4 + z_lo), core: 2. Of those that a mesh axis runs over, the one named last changes fastest.
Arguments:
- hidden: bfloat16 [65536, 8192], P(('replica', 'fsdp')), may hold values from -6 to 6
- key_cotangent: bfloat16 [65536, 512], P(('replica', 'fsdp')), may hold values from -0.15625 to 0.15625
- key_weight: float32 [8, 8192, 512], P('replica', 'fsdp'), may hold values from -0.0625 to 0.0625
- first_moment: float32 [8, 8192, 512], P('replica', 'fsdp'), may hold values from -4 to 4
- second_moment: float32 [8, 8192, 512], P('replica', 'fsdp'), may hold values from 0.01 to 1
- step_index: int32 [], replicated, may hold values from 1 to 1000
- anchor: float32 [8192, 512], P('fsdp'), may hold values from -6 to 6
- outer_momentum: float32 [8192, 512], P('fsdp'), may hold values from -6 to 6
- replica_fragment: bfloat16 [8, 8192, 512], P('replica', 'fsdp'), may hold values from -6 to 6
Outputs:
- new_weight: float32 [8, 8192, 512], P('replica', 'fsdp')
- new_first: float32 [8, 8192, 512], P('replica', 'fsdp')
- new_second: float32 [8, 8192, 512], P('replica', 'fsdp')
- new_anchor: float32 [8192, 512], P('fsdp')
- new_momentum: float32 [8192, 512], P('fsdp')
All inputs are finite; a program needn't handle non-finite values.
Results may differ from a plain program's by a relative error of at most 0.0003.
Values may be sent and summed in bfloat16 or wider, within the bound.
A program may use at most 64 MiB of HBM per device.

v0:
```python
import jax
import jax.numpy as jnp
from jax import lax
from jax.sharding import PartitionSpec as P


def body(
    hidden,
    key_cotangent,
    key_weight,
    first_moment,
    second_moment,
    step_index,
    anchor,
    outer_momentum,
    replica_fragment,
):
    replicas = lax.axis_size("replica")
    columns = lax.all_to_all(hidden, "fsdp", split_axis=1, concat_axis=0, tiled=True)
    grad = lax.dot_general(
        columns,
        lax.all_gather(key_cotangent, "fsdp", axis=0, tiled=True),
        (((0,), (0,)), ((), ())),
        preferred_element_type=jnp.float32,
    )[None]
    new_first = 0.9 * first_moment + 0.1 * grad
    new_second = 0.999 * second_moment + 0.001 * grad * grad
    steps = step_index.astype(jnp.float32)
    corr_one = 1.0 - jnp.power(jnp.float32(0.9), steps)
    corr_two = 1.0 - jnp.power(jnp.float32(0.999), steps)
    update = new_first / corr_one / (jnp.sqrt(new_second / corr_two) + 1e-08)
    new_weight = key_weight - 0.01 * (update + 0.1 * key_weight)
    differ = anchor - replica_fragment[0].astype(jnp.float32)
    delta = lax.psum(differ, "replica") / replicas
    new_momentum = 0.9 * outer_momentum + delta
    new_anchor = anchor - 0.7 * (delta + 0.9 * new_momentum)
    return (new_weight, new_first, new_second, new_anchor, new_momentum)


def solution(mesh):
    return jax.shard_map(
        body,
        mesh=mesh,
        in_specs=(
            P(("replica", "fsdp"), None),
            P(("replica", "fsdp"), None),
            P("replica", "fsdp", None),
            P("replica", "fsdp", None),
            P("replica", "fsdp", None),
            P(),
            P("fsdp", None),
            P("fsdp", None),
            P("replica", "fsdp", None),
        ),
        out_specs=(
            P("replica", "fsdp", None),
            P("replica", "fsdp", None),
            P("replica", "fsdp", None),
            P("fsdp", None),
            P("fsdp", None),
        ),
        check_vma=False,
    )
```

profile of v0, /device:TPU:6, one launch (start us, length us, event | category | flops | bytes accessed | tf_op | source)
XLA Modules:
  0.0 294.3 jit_solution(5303191868426134814)
XLA Ops:
  8.0 0.0 all-reduce.2.cloned.1.call-start
  8.0 1.7 convert_subtract_fusion
  9.8 0.0 all-reduce.2.cloned.1.call-update
  9.8 0.0 all-gather.2.cloned.1.call-start
  9.8 0.5 all-gather.2.cloned.1.call-update
  10.4 4.1 %copy.14 = bf16[128,8192]{0,1:T(8,128)(2,1)} copy(bf16[128,8192]{1,0:T(8,128)(2,1)} %param.9) | data formatting | bytes 4194304 | tf_op args[0]
  14.4 0.0 copy-start.1
  14.4 0.0 copy-start.5
  14.4 21.3 %all-to-all-start = ((bf16[128,64,128]{0,2,1:T(8,128)(2,1)}), bf16[128,64,128]{0,2,1:T(8,128)(2,1)S(1)}, u32[]{:S(2)}, u32[]{:S(2)}) async-start(bf16[128,64,128]{0,2,1:T(8,128)(2,1)} %bitcast.18), calls=%async_computation | async-start | bytes 4194304 | tf_op jit(solution)/shard_map/all_to_all | solution.py:19
  36.5 135.4 %all-reduce.2.cloned.1.call-done = f32[128,512]{1,0:T(8,128)} async-done(((f32[128,512]{1,0:T(8,128)}), f32[128,512]{1,0:T(8,128)}) %all-reduce.2.cloned.1.call-update) | async-done | bytes 262160 | tf_op jit(solution)/shard_map/psum | solution.py:34
  171.9 0.0 copy-done.1
  171.9 0.0 copy-done.5
  171.9 1.8 multiply_subtract_fusion
  173.7 0.0 all-to-all-done
  173.8 0.0 copy-start
  173.8 1.4 copy-done
  175.1 0.0 copy-start.2
  175.1 0.0 copy-start.3
  175.1 0.0 copy-start.4
  175.1 3.3 %copy.15 = bf16[64,128,128]{2,1,0:T(8,128)(2,1)S(1)} copy(bf16[64,128,128]{1,2,0:T(8,128)(2,1)} %bitcast.17) | data formatting | bytes 4194304 | tf_op jit(solution)/shard_map/all_to_all | solution.py:19
  178.4 102.7 %all-gather.2.cloned.1.call-done = bf16[8192,512]{1,0:T(8,128)(2,1)} async-done(((bf16[128,512]{1,0:T(8,128)(2,1)}), bf16[8192,512]{1,0:T(8,128)(2,1)}) %all-gather.2.cloned.1.call-update) | async-done | bytes 8388624 | tf_op jit(solution)/shard_map/all_gather | solution.py:22
  281.2 0.0 copy-done.2
  281.2 0.0 copy-done.3
  281.2 0.0 copy-done.4
  281.2 5.7 %multiply_subtract_fusion.1 = (f32[1,128,512]{2,1,0:T(8,128)}, f32[1,128,512]{2,1,0:T(8,128)}, f32[1,128,512]{2,1,0:T(8,128)}) fusion(f32[1,128,512]{2,1,0:T(8,128)S(1)} %copy-done.2, f32[]{:T(128)S(6)} %sub.16, f32[]{:T(128)S(6)} %sub.15, f32[1,128,512]{2,1,0:T(8,128)S(1)} %copy-done.3, f32[1,128,512]{2,1,0:T(8,128)S(1)} %copy-done.4, ...), kind=kOutput, calls=%fused_computation.7 | convolution fusion | flops 1074724864 | bytes 12058632 | tf_op jit(solution)/shard_map/dot_general | solution.py:20
Async XLA Ops:
  8.0 163.9 %all-reduce.2.cloned.1.call-start = ((), (), s32[]{:S(2)}) async-start(), calls=%async_computation.2 | async-start | bytes 524288 | tf_op jit(solution)/shard_map/psum | solution.py:34
  9.8 271.4 %all-gather.2.cloned.1.call-start = ((), (), s32[]{:S(2)}) async-start(), calls=%async_computation.1 | async-start | bytes 8519680 | tf_op jit(solution)/shard_map/all_gather | solution.py:22
  14.4 157.5 %copy-start.1 = (f32[128,512]{1,0:T(8,128)S(1)}, f32[128,512]{1,0:T(8,128)}, u32[]{:S(2)}) copy-start(f32[128,512]{1,0:T(8,128)} %param.15) | copy-start | bytes 786436
  14.4 157.5 %copy-start.5 = (f32[128,512]{1,0:T(8,128)S(1)}, f32[128,512]{1,0:T(8,128)}, u32[]{:S(2)}) copy-start(f32[128,512]{1,0:T(8,128)} %param.16) | copy-start | bytes 786436
  14.4 159.3 %all-to-all-start = ((bf16[128,64,128]{0,2,1:T(8,128)(2,1)}), bf16[128,64,128]{0,2,1:T(8,128)(2,1)S(1)}, u32[]{:S(2)}, u32[]{:S(2)}) async-start(bf16[128,64,128]{0,2,1:T(8,128)(2,1)} %bitcast.18), calls=%async_computation | async-start | bytes 4194304 | tf_op jit(solution)/shard_map/all_to_all | solution.py:19
  173.8 1.4 copy-start
  175.1 106.0 %copy-start.2 = (f32[1,128,512]{2,1,0:T(8,128)S(1)}, f32[1,128,512]{2,1,0:T(8,128)}, u32[]{:S(2)}) copy-start(f32[1,128,512]{2,1,0:T(8,128)} %param.11) | copy-start | bytes 786436
  175.1 106.0 %copy-start.3 = (f32[1,128,512]{2,1,0:T(8,128)S(1)}, f32[1,128,512]{2,1,0:T(8,128)}, u32[]{:S(2)}) copy-start(f32[1,128,512]{2,1,0:T(8,128)} %param.13) | copy-start | bytes 786436
  175.1 106.0 %copy-start.4 = (f32[1,128,512]{2,1,0:T(8,128)S(1)}, f32[1,128,512]{2,1,0:T(8,128)}, u32[]{:S(2)}) copy-start(f32[1,128,512]{2,1,0:T(8,128)} %param.12) | copy-start | bytes 786436
Sparse Core Ops, SparseCore 0:
  12.3 159.5 all-reduce.1
Sparse Core Ops, SparseCore 1:
  14.4 266.7 all-gather.1
where the time goes:
time: 296 us; the launch traced here: 294 us
  waiting for transfers between devices  239 us (81%)
  starting transfers between devices  21.4 us (7%)
  between operations  16.2 us (5%)
  local copies, waits for them, and re-layouts  8.75 us (3%)
  matrix products  5.72 us (2%)
  other arithmetic  3.54 us (1%)
    psum x1, waiting for transfers between devices, body(): delta = lax.psum(differ, 'replica') / replicas  135 us
    all_gather x1, waiting for transfers between devices, body(): lax.all_gather(key_cotangent, 'fsdp', axis=0, tiled=True)  103 us
    all_to_all x1, starting transfers between devices, body(): lax.all_to_all(hidden, 'fsdp', split_axis=1, concat_axis=0, tiled=True)  21.3 us
  transfers between devices with their start and end apart: 3, of which 2 were waited for; matrix products, arithmetic and copies ran while one was open for 3% of the time, Pallas kernels for 0%

commit v1 on v0

--- a/solution.py
+++ b/solution.py
@@ -1,7 +1,163 @@
+import functools
+
 import jax
 import jax.numpy as jnp
 from jax import lax
+from jax.experimental import pallas as pl
+from jax.experimental.pallas import tpu as pltpu
 from jax.sharding import PartitionSpec as P
+
+MESH = pl.DeviceIdType.MESH
+STEPS = (2, 1, 3, 0)
+
+
+def exchange(
+    hidden, cotan, frag, anchor, grad, delta,
+    hbuf, cbuf, part, relay, fin, dpart, danchor, dsum,
+    local, hsend, hrecv, csend, crecv, zsend, zrecv, dsend, drecv,
+):
+    rep = lax.axis_index("replica")
+    row = lax.axis_index("fsdp")
+    zh, y, x = row // 16, (row // 4) % 4, row % 4
+
+    def plane(dy, dx):
+        return (rep, zh * 16 + ((y + dy) % 4) * 4 + (x + dx) % 4)
+
+    def along_z(dz):
+        return (rep, ((zh + dz) % 4) * 16 + y * 4 + x)
+
+    def other(j):
+        return ((rep + j) % 8, row)
+
+    def send(src, dst, ssem, rsem, device):
+        pltpu.make_async_remote_copy(
+            src_ref=src, dst_ref=dst, send_sem=ssem, recv_sem=rsem, device_id=device, device_id_type=MESH
+        ).start()
+
+    def wait(ref, sem):
+        pltpu.make_async_copy(ref, ref, sem).wait()
+
+    barrier = pltpu.get_barrier_semaphore()
+
+    @pl.loop(1, 16)
+    def _(k):
+        pl.semaphore_signal(barrier, inc=1, device_id=plane(k // 4, k % 4), device_id_type=MESH)
+
+    @pl.loop(1, 8)
+    def _(j):
+        pl.semaphore_signal(barrier, inc=1, device_id=other(j), device_id_type=MESH)
+
+    for dz in (1, 3):
+        pl.semaphore_signal(barrier, inc=1, device_id=along_z(dz), device_id_type=MESH)
+
+    def column(q, dy, dx):
+        start = ((zh + STEPS[q]) % 4) * 16 + ((y + dy) % 4) * 4 + (x + dx) % 4
+        return pl.ds(pl.multiple_of(start * 128, 128), 128)
+
+    mine = pl.ds(pl.multiple_of(rep * 16, 16), 16)
+    own = [pltpu.make_async_copy(cotan, cbuf.at[0, 0], local.at[0])]
+    own += [
+        pltpu.make_async_copy(hidden.at[:, column(q, 0, 0)], hbuf.at[q, pl.ds(0, 128)], local.at[1 + q])
+        for q in range(4)
+    ]
+    own += [
+        pltpu.make_async_copy(frag.at[0, mine], dpart.at[0], local.at[5]),
+        pltpu.make_async_copy(anchor.at[mine], danchor, local.at[6]),
+    ]
+    for copy in own:
+        copy.start()
+    pl.semaphore_wait(barrier, 24)
+
+    for d in (1, 3, 2):
+        send(cotan.at[pl.ds(0, 64)], cbuf.at[0, d, pl.ds(0, 64)], csend.at[0], crecv.at[0], plane(0, d))
+        send(cotan.at[pl.ds(64, 64)], cbuf.at[d, 0, pl.ds(64, 64)], csend.at[1], crecv.at[1], plane(d, 0))
+
+    @pl.loop(1, 8)
+    def _(j):
+        rows = pl.ds(pl.multiple_of(((rep + j) % 8) * 16, 16), 16)
+        send(frag.at[0, rows], dpart.at[j], dsend.at[0], drecv.at[0], other(j))
+
+    def features(q):
+        @pl.loop(1, 16)
+        def _(k):
+            dy, dx = k // 4, k % 4
+            send(
+                hidden.at[:, column(q, dy, dx)],
+                hbuf.at[q, pl.ds(pl.multiple_of(k * 128, 128), 128)],
+                hsend.at[q], hrecv.at[q], plane(dy, dx),
+            )
+
+    features(0)
+    own[0].wait()
+    wait(cbuf.at[0, pl.ds(1, 3), pl.ds(0, 64)], crecv.at[0])
+    for d in (1, 3, 2):
+        send(cbuf.at[0, :, pl.ds(0, 64)], cbuf.at[d, :, pl.ds(0, 64)], csend.at[2], crecv.at[2], plane(d, 0))
+    wait(cbuf.at[pl.ds(1, 3), 0, pl.ds(64, 64)], crecv.at[1])
+    for d in (1, 3, 2):
+        send(cbuf.at[:, 0, pl.ds(64, 64)], cbuf.at[:, d, pl.ds(64, 64)], csend.at[3], crecv.at[3], plane(0, d))
+    features(1)
+    features(2)
+    features(3)
+
+    for copy in own[5:]:
+        copy.wait()
+    wait(dpart.at[pl.ds(1, 7)], drecv.at[0])
+    total = danchor[...] - dpart[0].astype(jnp.float32)
+    for j in range(1, 8):
+        total += danchor[...] - dpart[j].astype(jnp.float32)
+    dsum[mine] = total / 8
+
+    @pl.loop(1, 8)
+    def _(j):
+        send(dsum.at[mine], dsum.at[mine], dsend.at[1], drecv.at[1], other(j))
+
+    wait(cbuf.at[pl.ds(1, 3), :, pl.ds(0, 64)], crecv.at[2])
+    wait(cbuf.at[:, pl.ds(1, 3), pl.ds(64, 64)], crecv.at[3])
+
+    def product(q):
+        own[1 + q].wait()
+        wait(hbuf.at[q, pl.ds(128, 1920)], hrecv.at[q])
+        left = hbuf[q]
+        for half in range(2):
+            right = cbuf[:, :, :, pl.ds(half * 256, 256)].reshape(2048, 256)
+            part[q, half] = lax.dot_general(
+                left, right, (((0,), (0,)), ((), ())), preferred_element_type=jnp.float32
+            )
+
+    product(0)
+    send(part.at[0, 0], relay.at[0], zsend.at[0], zrecv.at[0], along_z(1))
+    send(part.at[0, 1], relay.at[1], zsend.at[1], zrecv.at[1], along_z(3))
+    product(1)
+    send(part.at[1, 1], fin.at[1], zsend.at[2], zrecv.at[2], along_z(1))
+    product(2)
+    send(part.at[2, 0], fin.at[2], zsend.at[3], zrecv.at[3], along_z(3))
+    wait(relay.at[0], zrecv.at[0])
+    part[1, 0] += relay[0]
+    send(part.at[1, 0], fin.at[0], zsend.at[4], zrecv.at[4], along_z(1))
+    wait(relay.at[1], zrecv.at[1])
+    part[2, 1] += relay[1]
+    send(part.at[2, 1], fin.at[3], zsend.at[5], zrecv.at[5], along_z(3))
+    product(3)
+
+    wait(dsum.at[pl.ds(0, 112)], drecv.at[1])
+    delta[...] = dsum[...]
+    wait(fin.at[1], zrecv.at[2])
+    wait(fin.at[2], zrecv.at[3])
+    wait(fin.at[0], zrecv.at[4])
+    grad[:, pl.ds(0, 256)] = part[3, 0] + fin[0] + fin[2]
+    wait(fin.at[3], zrecv.at[5])
+    grad[:, pl.ds(256, 256)] = part[3, 1] + fin[1] + fin[3]
+
+    for q in range(4):
+        wait(hbuf.at[q, pl.ds(128, 1920)], hsend.at[q])
+    wait(cbuf.at[0, pl.ds(1, 3), pl.ds(0, 64)], csend.at[0])
+    wait(cbuf.at[pl.ds(1, 3), 0, pl.ds(64, 64)], csend.at[1])
+    wait(cbuf.at[pl.ds(1, 3), :, pl.ds(0, 64)], csend.at[2])
+    wait(cbuf.at[:, pl.ds(1, 3), pl.ds(64, 64)], csend.at[3])
+    for m in range(6):
+        wait(relay.at[0], zsend.at[m])
+    wait(dpart.at[pl.ds(1, 7)], dsend.at[0])
+    wait(dsum.at[pl.ds(0, 112)], dsend.at[1])
 
 
 def body(
@@ -15,14 +171,30 @@
     outer_momentum,
     replica_fragment,
 ):
-    replicas = lax.axis_size("replica")
-    columns = lax.all_to_all(hidden, "fsdp", split_axis=1, concat_axis=0, tiled=True)
-    grad = lax.dot_general(
-        columns,
-        lax.all_gather(key_cotangent, "fsdp", axis=0, tiled=True),
-        (((0,), (0,)), ((), ())),
-        preferred_element_type=jnp.float32,
-    )[None]
+    dma = pltpu.SemaphoreType.DMA
+    grad, delta = pl.pallas_call(
+        exchange,
+        out_shape=[jax.ShapeDtypeStruct((128, 512), jnp.float32)] * 2,
+        in_specs=[pl.BlockSpec(memory_space=pl.ANY)] * 4,
+        out_specs=[pl.BlockSpec(memory_space=pltpu.VMEM)] * 2,
+        scratch_shapes=[
+            pltpu.VMEM((4, 2048, 128), jnp.bfloat16),
+            pltpu.VMEM((4, 4, 128, 512), jnp.bfloat16),
+            pltpu.VMEM((4, 2, 128, 256), jnp.float32),
+            pltpu.VMEM((2, 128, 256), jnp.float32),
+            pltpu.VMEM((4, 128, 256), jnp.float32),
+            pltpu.VMEM((8, 16, 512), jnp.bfloat16),
+            pltpu.VMEM((16, 512), jnp.float32),
+            pltpu.VMEM((128, 512), jnp.float32),
+            dma((7,)), dma((4,)), dma((4,)), dma((4,)), dma((4,)), dma((6,)), dma((6,)), dma((2,)), dma((2,)),
+        ],
+        compiler_params=pltpu.CompilerParams(
+            collective_id=0, has_side_effects=True, vmem_limit_bytes=40 * 1024 * 1024
+        ),
+        cost_estimate=pl.CostEstimate(flops=2 * 2048 * 512 * 512, bytes_accessed=8 << 20, transcendentals=0),
+        name="exchange",
+    )(hidden, key_cotangent, replica_fragment, anchor)
+    grad = grad[None]
     new_first = 0.9 * first_moment + 0.1 * grad
     new_second = 0.999 * second_moment + 0.001 * grad * grad
     steps = step_index.astype(jnp.float32)
@@ -30,8 +202,6 @@
     corr_two = 1.0 - jnp.power(jnp.float32(0.999), steps)
     update = new_first / corr_one / (jnp.sqrt(new_second / corr_two) + 1e-08)
     new_weight = key_weight - 0.01 * (update + 0.1 * key_weight)
-    differ = anchor - replica_fragment[0].astype(jnp.float32)
-    delta = lax.psum(differ, "replica") / replicas
     new_momentum = 0.9 * outer_momentum + delta
     new_anchor = anchor - 0.7 * (delta + 0.9 * new_momentum)
     return (new_weight, new_first, new_second, new_anchor, new_momentum)

time: 296 us -> 82.9 us (0.28)
  waiting for transfers between devices: 239 us -> 0 us
  Pallas kernels: 0 us -> 74.8 us
  starting transfers between devices: 21.4 us -> 0 us
  between operations: 16.2 us -> 1.41 us
  matrix products: 5.72 us -> 0 us
  local copies, waits for them, and re-layouts: 8.75 us -> 4.36 us
    psum x1 -> x0, waiting for transfers between devices: 135 us -> none  [body(): delta = lax.psum(differ, 'replica') / replicas]
    all_gather x1 -> x0, waiting for transfers between devices: 103 us -> none  [body(): lax.all_gather(key_cotangent, 'fsdp', axis=0, tiled=True)]
    pallas_call x0 -> x1, Pallas kernels: none -> 74.8 us  [body(): pl.pallas_call(exchange, out_shape=[jax.ShapeDtypeStruct((128, 512), jnp....]
    all_to_all x1 -> x0, starting transfers between devices: 21.3 us -> none  [body(): lax.all_to_all(hidden, 'fsdp', split_axis=1, concat_axis=0, tiled=True)]
    dot_general x1 -> x0, matrix products: 5.72 us -> none  [body(): lax.dot_general(columns, lax.all_gather(key_cotangent, 'fsdp', axis=0, ti...]
    all_to_all x1 -> x0, local copies, waits for them, and re-layouts: 3.29 us -> none  [body(): lax.all_to_all(hidden, 'fsdp', split_axis=1, concat_axis=0, tiled=True)]
  transfers between devices with their start and end apart: 3 -> 0, of which waited for: 2 -> 0; matrix products, arithmetic and copies ran while one was open for 3% -> 0% of each run, Pallas kernels for 0% -> 0%
where the time goes in v1:
time: 82.9 us; the launch traced here: 82.4 us
  Pallas kernels  74.8 us (90%)
  local copies, waits for them, and re-layouts  4.36 us (5%)
  other arithmetic  1.86 us (2%)
  between operations  1.41 us (2%)
    pallas_call x1, Pallas kernels, body(): pl.pallas_call(exchange, out_shape=[jax.ShapeDtypeStruct((128, 512), jnp....  74.8 us
    unnamed x16, local copies, waits for them, and re-layouts  4.36 us

profile of v1, /device:TPU:6, one launch (start us, length us, event | category | flops | bytes accessed | tf_op | source)
XLA Modules:
  0.0 82.4 jit_solution(5485737681274325365)
XLA Ops:
  1.4 0.0 copy-start
  1.4 0.9 %copy-done = f32[128,512]{1,0:T(8,128)S(1)} copy-done((f32[128,512]{1,0:T(8,128)S(1)}, f32[128,512]{1,0:T(8,128)}, u32[]{:S(2)}) %copy-start) | copy-done | bytes 262168
  2.3 0.0 copy-start.1
  2.3 1.6 %copy-done.1 = bf16[128,8192]{1,0:T(8,128)(2,1)S(1)} copy-done((bf16[128,8192]{1,0:T(8,128)(2,1)S(1)}, bf16[128,8192]{1,0:T(8,128)(2,1)}, u32[]{:S(2)}) %copy-start.1) | copy-done | bytes 2097176
  3.9 0.0 copy-start.2
  3.9 0.9 %copy-done.2 = bf16[128,512]{1,0:T(8,128)(2,1)S(1)} copy-done((bf16[128,512]{1,0:T(8,128)(2,1)S(1)}, bf16[128,512]{1,0:T(8,128)(2,1)}, u32[]{:S(2)}) %copy-start.2) | copy-done | bytes 131096
  4.8 0.0 copy-start.3
  4.8 0.9 %copy-done.3 = bf16[1,128,512]{2,1,0:T(8,128)(2,1)S(1)} copy-done((bf16[1,128,512]{2,1,0:T(8,128)(2,1)S(1)}, bf16[1,128,512]{2,1,0:T(8,128)(2,1)}, u32[]{:S(2)}) %copy-start.3) | copy-done | bytes 131096
  5.7 0.0 copy-start.4
  5.7 0.0 copy-start.5
  5.7 0.0 copy-start.6
  5.7 0.0 copy-start.7
  5.7 74.8 %exchange.1 = (f32[128,512]{1,0:T(8,128)S(1)}, f32[128,512]{1,0:T(8,128)S(1)}) custom-call(bf16[128,8192]{1,0:T(8,128)(2,1)S(1)} %copy-done.1, bf16[128,512]{1,0:T(8,128)(2,1)S(1)} %copy-done.2, bf16[1,128,512]{2,1,0:T(8,128)(2,1)S(1)} %copy-done.3, f32[128,512]{1,0:T(8,128)S(1)} %copy-done), custom_call_target="tpu_custom_call" | custom-call | flops 1073741824 | bytes 8388608 | tf_op jit(solution)/shard_map/exchange/pallas_call | solution.py:175
  80.5 0.0 copy-done.4
  80.5 0.0 copy-done.5
  80.6 0.0 copy-done.6
  80.6 1.0 %multiply_subtract_fusion.1 = (f32[1,128,512]{2,1,0:T(8,128)}, f32[1,128,512]{2,1,0:T(8,128)}, f32[1,128,512]{2,1,0:T(8,128)}) fusion(f32[1,128,512]{2,1,0:T(8,128)S(1)} %copy-done.4, f32[]{:T(128)S(6)} %sub.13, f32[]{:T(128)S(6)} %sub.12, f32[128,512]{1,0:T(8,128)S(1)} %get-tuple-element.7, f32[1,128,512]{2,1,0:T(8,128)S(1)} %copy-done.5, ...), kind=kLoop, calls=%fused_computation.6 | loop fusion | flops 983040 | bytes 1835016 | tf_op jit(solution)/shard_map/sub | solution.py:204
  81.6 0.0 copy-done.7
  81.6 0.9 %multiply_subtract_fusion = (f32[128,512]{1,0:T(8,128)}, f32[128,512]{1,0:T(8,128)}) fusion(f32[128,512]{1,0:T(8,128)S(1)} %copy-done, f32[128,512]{1,0:T(8,128)S(1)} %get-tuple-element.8, f32[128,512]{1,0:T(8,128)S(1)} %copy-done.7), kind=kLoop, calls=%fused_computation.4 | loop fusion | flops 393216 | bytes 1310720 | tf_op jit(solution)/shard_map/sub | solution.py:206
Async XLA Ops:
  1.4 1.0 %copy-start = (f32[128,512]{1,0:T(8,128)S(1)}, f32[128,512]{1,0:T(8,128)}, u32[]{:S(2)}) copy-start(f32[128,512]{1,0:T(8,128)} %anchor.1) | copy-start | bytes 786436
  2.3 1.6 %copy-start.1 = (bf16[128,8192]{1,0:T(8,128)(2,1)S(1)}, bf16[128,8192]{1,0:T(8,128)(2,1)}, u32[]{:S(2)}) copy-start(bf16[128,8192]{1,0:T(8,128)(2,1)} %hidden.1) | copy-start | bytes 6291460
  3.9 0.9 %copy-start.2 = (bf16[128,512]{1,0:T(8,128)(2,1)S(1)}, bf16[128,512]{1,0:T(8,128)(2,1)}, u32[]{:S(2)}) copy-start(bf16[128,512]{1,0:T(8,128)(2,1)} %cotan.1) | copy-start | bytes 393220
  4.8 0.9 %copy-start.3 = (bf16[1,128,512]{2,1,0:T(8,128)(2,1)S(1)}, bf16[1,128,512]{2,1,0:T(8,128)(2,1)}, u32[]{:S(2)}) copy-start(bf16[1,128,512]{2,1,0:T(8,128)(2,1)} %frag.1) | copy-start | bytes 393220
  5.7 74.8 %copy-start.4 = (f32[1,128,512]{2,1,0:T(8,128)S(1)}, f32[1,128,512]{2,1,0:T(8,128)}, u32[]{:S(2)}) copy-start(f32[1,128,512]{2,1,0:T(8,128)} %param.11) | copy-start | bytes 786436
  5.7 74.8 %copy-start.5 = (f32[1,128,512]{2,1,0:T(8,128)S(1)}, f32[1,128,512]{2,1,0:T(8,128)}, u32[]{:S(2)}) copy-start(f32[1,128,512]{2,1,0:T(8,128)} %param.13) | copy-start | bytes 786436
  5.7 74.8 %copy-start.6 = (f32[1,128,512]{2,1,0:T(8,128)S(1)}, f32[1,128,512]{2,1,0:T(8,128)}, u32[]{:S(2)}) copy-start(f32[1,128,512]{2,1,0:T(8,128)} %param.12) | copy-start | bytes 786436
  5.7 75.8 %copy-start.7 = (f32[128,512]{1,0:T(8,128)S(1)}, f32[128,512]{1,0:T(8,128)}, u32[]{:S(2)}) copy-start(f32[128,512]{1,0:T(8,128)} %param.16) | copy-start | bytes 786436

commit v2 on v1

--- a/solution.py
+++ b/solution.py
@@ -13,8 +13,8 @@
 
 def exchange(
     hidden, cotan, frag, anchor, grad, delta,
-    hbuf, cbuf, part, relay, fin, dpart, danchor, dsum,
-    local, hsend, hrecv, csend, crecv, zsend, zrecv, dsend, drecv,
+    hbuf, cbuf, part, code, gain, recode, regain, dpart, danchor, dsum,
+    local, hsend, hrecv, csend, crecv, zsend, zrecv, dsend, drecv, ready,
 ):
     rep = lax.axis_index("replica")
     row = lax.axis_index("fsdp")
@@ -37,18 +37,23 @@
     def wait(ref, sem):
         pltpu.make_async_copy(ref, ref, sem).wait()
 
+    up, down = (zh + 1) % 4, (zh + 3) % 4
     barrier = pltpu.get_barrier_semaphore()
 
     @pl.loop(1, 16)
     def _(k):
         pl.semaphore_signal(barrier, inc=1, device_id=plane(k // 4, k % 4), device_id_type=MESH)
 
-    @pl.loop(1, 8)
-    def _(j):
-        pl.semaphore_signal(barrier, inc=1, device_id=other(j), device_id_type=MESH)
-
-    for dz in (1, 3):
-        pl.semaphore_signal(barrier, inc=1, device_id=along_z(dz), device_id_type=MESH)
+    @pl.loop(rep + 1, 8)
+    def _(r):
+        pl.semaphore_signal(barrier, inc=1, device_id=(r, row), device_id_type=MESH)
+
+    for dz, at in ((1, up), (3, down)):
+        @pl.when(at > zh)
+        def _():
+            pl.semaphore_signal(barrier, inc=1, device_id=along_z(dz), device_id_type=MESH)
+
+    lower = (up < zh).astype(jnp.int32) + (down < zh).astype(jnp.int32)
 
     def column(q, dy, dx):
         start = ((zh + STEPS[q]) % 4) * 16 + ((y + dy) % 4) * 4 + (x + dx) % 4
@@ -66,16 +71,20 @@
     ]
     for copy in own:
         copy.start()
-    pl.semaphore_wait(barrier, 24)
+    pl.semaphore_wait(barrier, 15 + rep + lower)
+
+    @pl.loop(0, rep)
+    def _(r):
+        pl.semaphore_signal(ready.at[0], inc=1, device_id=(r, row), device_id_type=MESH)
+
+    for dz, at in ((1, up), (3, down)):
+        @pl.when(at < zh)
+        def _():
+            pl.semaphore_signal(ready.at[1], inc=1, device_id=along_z(dz), device_id_type=MESH)
 
     for d in (1, 3, 2):
         send(cotan.at[pl.ds(0, 64)], cbuf.at[0, d, pl.ds(0, 64)], csend.at[0], crecv.at[0], plane(0, d))
         send(cotan.at[pl.ds(64, 64)], cbuf.at[d, 0, pl.ds(64, 64)], csend.at[1], crecv.at[1], plane(d, 0))
-
-    @pl.loop(1, 8)
-    def _(j):
-        rows = pl.ds(pl.multiple_of(((rep + j) % 8) * 16, 16), 16)
-        send(frag.at[0, rows], dpart.at[j], dsend.at[0], drecv.at[0], other(j))
 
     def features(q):
         @pl.loop(1, 16)
@@ -88,6 +97,16 @@
             )
 
     features(0)
+
+    @pl.when(rep < 7)
+    def _():
+        pl.semaphore_wait(ready.at[0], 7 - rep)
+
+    @pl.loop(1, 8)
+    def _(j):
+        rows = pl.ds(pl.multiple_of(((rep + j) % 8) * 16, 16), 16)
+        send(frag.at[0, rows], dpart.at[j], dsend.at[0], drecv.at[0], other(j))
+
     own[0].wait()
     wait(cbuf.at[0, pl.ds(1, 3), pl.ds(0, 64)], crecv.at[0])
     for d in (1, 3, 2):
@@ -95,9 +114,9 @@
     wait(cbuf.at[pl.ds(1, 3), 0, pl.ds(64, 64)], crecv.at[1])
     for d in (1, 3, 2):
         send(cbuf.at[:, 0, pl.ds(64, 64)], cbuf.at[:, d, pl.ds(64, 64)], csend.at[3], crecv.at[3], plane(0, d))
+    own[1].wait()
+    wait(hbuf.at[0, pl.ds(128, 1920)], hrecv.at[0])
     features(1)
-    features(2)
-    features(3)
 
     for copy in own[5:]:
         copy.wait()
@@ -107,16 +126,20 @@
         total += danchor[...] - dpart[j].astype(jnp.float32)
     dsum[mine] = total / 8
 
-    @pl.loop(1, 8)
-    def _(j):
+    for j in (2, 4, 6):
         send(dsum.at[mine], dsum.at[mine], dsend.at[1], drecv.at[1], other(j))
+    sibling = (rep + 1 - 2 * (rep % 2), row)
+    send(dsum.at[mine], dsum.at[mine], dsend.at[2], drecv.at[2], sibling)
 
     wait(cbuf.at[pl.ds(1, 3), :, pl.ds(0, 64)], crecv.at[2])
     wait(cbuf.at[:, pl.ds(1, 3), pl.ds(64, 64)], crecv.at[3])
 
     def product(q):
-        own[1 + q].wait()
-        wait(hbuf.at[q, pl.ds(128, 1920)], hrecv.at[q])
+        if q:
+            own[1 + q].wait()
+            wait(hbuf.at[q, pl.ds(128, 1920)], hrecv.at[q])
+        if q < 2:
+            features(q + 2)
         left = hbuf[q]
         for half in range(2):
             right = cbuf[:, :, :, pl.ds(half * 256, 256)].reshape(2048, 256)
@@ -124,29 +147,44 @@
                 left, right, (((0,), (0,)), ((), ())), preferred_element_type=jnp.float32
             )
 
+    def pass_on(m, value, dz):
+        top = jnp.maximum(jnp.max(jnp.abs(value), axis=0, keepdims=True), 1e-30)
+        code[m] = jnp.round(value * (32767.0 / top)).astype(jnp.int32).astype(jnp.int16)
+        gain[m] = jnp.broadcast_to(top, (8, 256))
+        send(code.at[m], recode.at[m], zsend.at[m], zrecv.at[m], along_z(dz))
+        send(gain.at[m], regain.at[m], zsend.at[6 + m], zrecv.at[6 + m], along_z(dz))
+
+    def received(m):
+        wait(recode.at[m], zrecv.at[m])
+        wait(regain.at[m], zrecv.at[6 + m])
+        return recode[m].astype(jnp.int32).astype(jnp.float32) * (regain[m, 0:1] * (1.0 / 32767.0))
+
     product(0)
-    send(part.at[0, 0], relay.at[0], zsend.at[0], zrecv.at[0], along_z(1))
-    send(part.at[0, 1], relay.at[1], zsend.at[1], zrecv.at[1], along_z(3))
+    @pl.when(lower < 2)
+    def _():
+        pl.semaphore_wait(ready.at[1], 2 - lower)
+
+    pass_on(0, part[0, 0], 1)
+    pass_on(1, part[0, 1], 3)
     product(1)
-    send(part.at[1, 1], fin.at[1], zsend.at[2], zrecv.at[2], along_z(1))
+    pass_on(2, part[1, 1], 1)
     product(2)
-    send(part.at[2, 0], fin.at[2], zsend.at[3], zrecv.at[3], along_z(3))
-    wait(relay.at[0], zrecv.at[0])
-    part[1, 0] += relay[0]
-    send(part.at[1, 0], fin.at[0], zsend.at[4], zrecv.at[4], along_z(1))
-    wait(relay.at[1], zrecv.at[1])
-    part[2, 1] += relay[1]
-    send(part.at[2, 1], fin.at[3], zsend.at[5], zrecv.at[5], along_z(3))
+    pass_on(3, part[2, 0], 3)
+    wait(dsum.at[pl.ds(0, 48)], drecv.at[1])
+    for j in (2, 4, 6):
+        there = pl.ds(pl.multiple_of(((rep + j) % 8) * 16, 16), 16)
+        send(dsum.at[there], dsum.at[there], dsend.at[3], drecv.at[3], sibling)
+    pass_on(4, part[1, 0] + received(0), 1)
+    pass_on(5, part[2, 1] + received(1), 3)
     product(3)
 
-    wait(dsum.at[pl.ds(0, 112)], drecv.at[1])
+    wait(dsum.at[pl.ds(0, 16)], drecv.at[2])
+    wait(dsum.at[pl.ds(0, 48)], drecv.at[3])
     delta[...] = dsum[...]
-    wait(fin.at[1], zrecv.at[2])
-    wait(fin.at[2], zrecv.at[3])
-    wait(fin.at[0], zrecv.at[4])
-    grad[:, pl.ds(0, 256)] = part[3, 0] + fin[0] + fin[2]
-    wait(fin.at[3], zrecv.at[5])
-    grad[:, pl.ds(256, 256)] = part[3, 1] + fin[1] + fin[3]
+    part[3, 1] += received(2)
+    part[3, 0] += received(3)
+    grad[:, pl.ds(0, 256)] = part[3, 0] + received(4)
+    grad[:, pl.ds(256, 256)] = part[3, 1] + received(5)
 
     for q in range(4):
         wait(hbuf.at[q, pl.ds(128, 1920)], hsend.at[q])
@@ -155,9 +193,12 @@
     wait(cbuf.at[pl.ds(1, 3), :, pl.ds(0, 64)], csend.at[2])
     wait(cbuf.at[:, pl.ds(1, 3), pl.ds(64, 64)], csend.at[3])
     for m in range(6):
-        wait(relay.at[0], zsend.at[m])
+        wait(code.at[m], zsend.at[m])
+        wait(gain.at[m], zsend.at[6 + m])
     wait(dpart.at[pl.ds(1, 7)], dsend.at[0])
-    wait(dsum.at[pl.ds(0, 112)], dsend.at[1])
+    wait(dsum.at[pl.ds(0, 48)], dsend.at[1])
+    wait(dsum.at[pl.ds(0, 16)], dsend.at[2])
+    wait(dsum.at[pl.ds(0, 48)], dsend.at[3])
 
 
 def body(
@@ -181,15 +222,18 @@
             pltpu.VMEM((4, 2048, 128), jnp.bfloat16),
             pltpu.VMEM((4, 4, 128, 512), jnp.bfloat16),
             pltpu.VMEM((4, 2, 128, 256), jnp.float32),
-            pltpu.VMEM((2, 128, 256), jnp.float32),
-            pltpu.VMEM((4, 128, 256), jnp.float32),
+            pltpu.VMEM((6, 128, 256), jnp.int16),
+            pltpu.VMEM((6, 8, 256), jnp.float32),
+            pltpu.VMEM((6, 128, 256), jnp.int16),
+            pltpu.VMEM((6, 8, 256), jnp.float32),
             pltpu.VMEM((8, 16, 512), jnp.bfloat16),
             pltpu.VMEM((16, 512), jnp.float32),
             pltpu.VMEM((128, 512), jnp.float32),
-            dma((7,)), dma((4,)), dma((4,)), dma((4,)), dma((4,)), dma((6,)), dma((6,)), dma((2,)), dma((2,)),
+            dma((7,)), dma((4,)), dma((4,)), dma((4,)), dma((4,)), dma((12,)), dma((12,)), dma((4,)), dma((4,)),
+            pltpu.SemaphoreType.REGULAR((2,)),
         ],
         compiler_params=pltpu.CompilerParams(
-            collective_id=0, has_side_effects=True, vmem_limit_bytes=40 * 1024 * 1024
+            collective_id=0, has_side_effects=True, vmem_limit_bytes=60 * 1024 * 1024
         ),
         cost_estimate=pl.CostEstimate(flops=2 * 2048 * 512 * 512, bytes_accessed=8 << 20, transcendentals=0),
         name="exchange",

time: 82.9 us -> 67.4 us (0.81)
  Pallas kernels: 74.8 us -> 61.7 us
  local copies, waits for them, and re-layouts: 4.36 us -> 0.02 us
  other arithmetic: 1.86 us -> 3.76 us
    pallas_call x1, Pallas kernels: 74.8 us -> 61.7 us  [body(): pl.pallas_call(exchange, out_shape=[jax.ShapeDtypeStruct((128, 512), jnp....]
    unnamed x16 -> x10, local copies, waits for them, and re-layouts: 4.36 us -> 0.02 us
    sub x1, other arithmetic: 0.86 us -> 1.82 us  [body(): new_anchor = anchor - 0.7 * (delta + 0.9 * new_momentum)]
    sub x1, other arithmetic: 1 us -> 1.95 us  [body(): new_weight = key_weight - 0.01 * (update + 0.1 * key_weight)]
where the time goes in v2:
time: 67.4 us; the launch traced here: 67 us
  Pallas kernels  61.7 us (92%)
  other arithmetic  3.76 us (6%)
  between operations  1.51 us (2%)
    pallas_call x1, Pallas kernels, body(): pl.pallas_call(exchange, out_shape=[jax.ShapeDtypeStruct((128, 512), jnp....  61.7 us
    sub x1, other arithmetic, body(): new_weight = key_weight - 0.01 * (update + 0.1 * key_weight)  1.95 us
    sub x1, other arithmetic, body(): new_anchor = anchor - 0.7 * (delta + 0.9 * new_momentum)  1.82 us

profile of v2, /device:TPU:6, one launch (start us, length us, event | category | flops | bytes accessed | tf_op | source)
XLA Modules:
  0.0 67.0 jit_solution(10200595079006953600)
XLA Ops:
  0.6 0.0 copy-start.1
  0.6 0.0 copy-start.2
  0.7 0.0 copy-start
  1.5 0.0 copy-start.3
  1.5 0.0 copy-start.4
  1.5 61.7 %exchange.1 = (f32[128,512]{1,0:T(8,128)}, f32[128,512]{1,0:T(8,128)}) custom-call(bf16[128,8192]{1,0:T(8,128)(2,1)} %hidden.1, bf16[128,512]{1,0:T(8,128)(2,1)} %cotan.1, bf16[1,128,512]{2,1,0:T(8,128)(2,1)} %frag.1, f32[128,512]{1,0:T(8,128)} %anchor.1), custom_call_target="tpu_custom_call" | custom-call | flops 1073741824 | bytes 8388608 | tf_op jit(solution)/shard_map/exchange/pallas_call | solution.py:216
  63.2 0.0 copy-done.1
  63.2 0.0 copy-done.2
  63.2 0.0 copy-done
  63.2 1.9 %multiply_subtract_fusion.1 = (f32[1,128,512]{2,1,0:T(8,128)}, f32[1,128,512]{2,1,0:T(8,128)}, f32[1,128,512]{2,1,0:T(8,128)}) fusion(f32[1,128,512]{2,1,0:T(8,128)S(1)} %copy-done, f32[]{:T(128)S(6)} %sub.13, f32[]{:T(128)S(6)} %sub.12, f32[128,512]{1,0:T(8,128)} %get-tuple-element.7, f32[1,128,512]{2,1,0:T(8,128)S(1)} %copy-done.1, ...), kind=kLoop, calls=%fused_computation.6 | loop fusion | flops 983040 | bytes 1835016 | tf_op jit(solution)/shard_map/sub | solution.py:248
  65.1 0.0 copy-done.3
  65.1 0.0 copy-done.4
  65.2 1.8 %multiply_subtract_fusion = (f32[128,512]{1,0:T(8,128)}, f32[128,512]{1,0:T(8,128)}) fusion(f32[128,512]{1,0:T(8,128)S(1)} %copy-done.3, f32[128,512]{1,0:T(8,128)} %get-tuple-element.8, f32[128,512]{1,0:T(8,128)S(1)} %copy-done.4), kind=kLoop, calls=%fused_computation.4 | loop fusion | flops 393216 | bytes 1310720 | tf_op jit(solution)/shard_map/sub | solution.py:250
Async XLA Ops:
  0.6 62.5 %copy-start.1 = (f32[1,128,512]{2,1,0:T(8,128)S(1)}, f32[1,128,512]{2,1,0:T(8,128)}, u32[]{:S(2)}) copy-start(f32[1,128,512]{2,1,0:T(8,128)} %param.13) | copy-start | bytes 786436
  0.6 62.5 %copy-start.2 = (f32[1,128,512]{2,1,0:T(8,128)S(1)}, f32[1,128,512]{2,1,0:T(8,128)}, u32[]{:S(2)}) copy-start(f32[1,128,512]{2,1,0:T(8,128)} %param.12) | copy-start | bytes 786436
  0.7 62.5 %copy-start = (f32[1,128,512]{2,1,0:T(8,128)S(1)}, f32[1,128,512]{2,1,0:T(8,128)}, u32[]{:S(2)}) copy-start(f32[1,128,512]{2,1,0:T(8,128)} %param.11) | copy-start | bytes 786436
  1.5 63.7 %copy-start.3 = (f32[128,512]{1,0:T(8,128)S(1)}, f32[128,512]{1,0:T(8,128)}, u32[]{:S(2)}) copy-start(f32[128,512]{1,0:T(8,128)} %anchor.1) | copy-start | bytes 786436
  1.5 63.7 %copy-start.4 = (f32[128,512]{1,0:T(8,128)S(1)}, f32[128,512]{1,0:T(8,128)}, u32[]{:S(2)}) copy-start(f32[128,512]{1,0:T(8,128)} %param.16) | copy-start | bytes 786436

commit v3 on v2

v3 whole, which is shorter than its diff:
```python
import functools

import jax
import jax.numpy as jnp
from jax import lax
from jax.experimental import pallas as pl
from jax.experimental.pallas import tpu as pltpu
from jax.sharding import PartitionSpec as P

MESH = pl.DeviceIdType.MESH
STEPS = (2, 1, 3, 0)
BY_X = (True, False, False, True)


def exchange(
    hidden, cotan, frag, anchor, grad, delta,
    hbuf, cbuf, ycode, ygain, yrecode, yregain, part, code, gain, recode, regain, dpart, danchor, dsum,
    local, hsend, hrecv, csend, crecv, ysend, yrecv, zsend, zrecv, dsend, drecv, ready,
):
    rep = lax.axis_index("replica")
    row = lax.axis_index("fsdp")
    zh, y, x = row // 16, (row // 4) % 4, row % 4

    def along_x(dx):
        return (rep, zh * 16 + y * 4 + (x + dx) % 4)

    def along_y(dy):
        return (rep, zh * 16 + ((y + dy) % 4) * 4 + x)

    def along_z(dz):
        return (rep, ((zh + dz) % 4) * 16 + y * 4 + x)

    def other(j):
        return ((rep + j) % 8, row)

    def send(src, dst, ssem, rsem, device):
        pltpu.make_async_remote_copy(
            src_ref=src, dst_ref=dst, send_sem=ssem, recv_sem=rsem, device_id=device, device_id_type=MESH
        ).start()

    def wait(ref, sem):
        pltpu.make_async_copy(ref, ref, sem).wait()

    up, down = (zh + 1) % 4, (zh + 3) % 4
    barrier = pltpu.get_barrier_semaphore()
    for d in (1, 2, 3):
        pl.semaphore_signal(barrier, inc=1, device_id=along_x(d), device_id_type=MESH)
        pl.semaphore_signal(barrier, inc=1, device_id=along_y(d), device_id_type=MESH)

    @pl.loop(rep + 1, 8)
    def _(r):
        pl.semaphore_signal(barrier, inc=1, device_id=(r, row), device_id_type=MESH)

    for dz, at in ((1, up), (3, down)):
        @pl.when(at > zh)
        def _():
            pl.semaphore_signal(barrier, inc=1, device_id=along_z(dz), device_id_type=MESH)

    lower = (up < zh).astype(jnp.int32) + (down < zh).astype(jnp.int32)

    def block(q, b, a):
        dy, dx = (b, a) if BY_X[q] else (a, b)
        start = ((zh + STEPS[q]) % 4) * 16 + ((y + dy) % 4) * 4 + (x + dx) % 4
        return hidden.at[:, pl.ds(pl.multiple_of(start * 128, 128), 128)]

    def place(q, b, a):
        return hbuf.at[q, pl.ds(pl.multiple_of(a * 128, 128), 128), pl.ds(pl.multiple_of(b * 128, 128), 128)]

    mine = pl.ds(pl.multiple_of(rep * 16, 16), 16)
    shared = [
        pltpu.make_async_copy(cotan, cbuf.at[0, pl.ds(0, 128)], local.at[4]),
        pltpu.make_async_copy(cotan, cbuf.at[1, pl.ds(0, 128)], local.at[7]),
        pltpu.make_async_copy(frag.at[0, mine], dpart.at[0], local.at[5]),
        pltpu.make_async_copy(anchor.at[mine], danchor, local.at[6]),
    ]
    for copy in shared:
        copy.start()
    for q in range(4):
        @pl.loop(0, 4)
        def _(b):
            pltpu.make_async_copy(block(q, b, 0), place(q, b, 0), local.at[q]).start()

    pl.semaphore_wait(barrier, 6 + rep + lower)

    @pl.loop(0, rep)
    def _(r):
        pl.semaphore_signal(ready.at[0], inc=1, device_id=(r, row), device_id_type=MESH)

    for dz, at in ((1, up), (3, down)):
        @pl.when(at < zh)
        def _():
            pl.semaphore_signal(ready.at[1], inc=1, device_id=along_z(dz), device_id_type=MESH)

    for d in (1, 3, 2):
        send(cotan, cbuf.at[0, pl.ds(d * 128, 128)], csend.at[0], crecv.at[0], along_x(d))
        send(cotan, cbuf.at[1, pl.ds(d * 128, 128)], csend.at[1], crecv.at[1], along_y(d))

    def features(q):
        @pl.loop(0, 12)
        def _(k):
            a, b = 1 + k // 4, k % 4
            device = along_x(a) if BY_X[q] else along_y(a)
            send(block(q, b, a), place(q, b, a), hsend.at[q], hrecv.at[q], device)

    def sent(q):
        wait(hbuf.at[q, pl.ds(128, 384)], hsend.at[q])

    features(0)
    features(1)

    @pl.when(rep < 7)
    def _():
        pl.semaphore_wait(ready.at[0], 7 - rep)

    @pl.loop(1, 8)
    def _(j):
        rows = pl.ds(pl.multiple_of(((rep + j) % 8) * 16, 16), 16)
        send(frag.at[0, rows], dpart.at[j], dsend.at[0], drecv.at[0], other(j))

    def encode(value, codes, tops):
        top = jnp.maximum(jnp.max(jnp.abs(value), axis=0, keepdims=True), 1e-30)
        codes[...] = jnp.round(value * (32767.0 / top)).astype(jnp.int32).astype(jnp.int16)
        for c in range(top.shape[1] // 128):
            tops[pl.ds(c, 1)] = top[:, c * 128 : c * 128 + 128]

    def decode(codes, tops):
        top = jnp.concatenate([tops[pl.ds(c, 1)] for c in range(tops.shape[0])], axis=1)
        return codes[...].astype(jnp.int32).astype(jnp.float32) * (top * (1.0 / 32767.0))

    def product(q, b):
        left = hbuf[q, :, pl.ds(pl.multiple_of(b * 128, 128), 128)]
        right = cbuf[0 if BY_X[q] else 1]
        return lax.dot_general(left, right, (((0,), (0,)), ((), ())), preferred_element_type=jnp.float32)

    def scatter(q):
        wait(hbuf.at[q, pl.ds(0, 128)], local.at[q])
        wait(hbuf.at[q, pl.ds(128, 384)], hrecv.at[q])

        @pl.loop(1, 4)
        def _(b):
            encode(product(q, b), ycode.at[q, b - 1], ygain.at[q, b - 1])
            device = along_y(b) if BY_X[q] else along_x(b)
            send(ycode.at[q, b - 1], yrecode.at[q, b - 1], ysend.at[0, q], yrecv.at[0, q], device)
            send(ygain.at[q, b - 1], yregain.at[q, b - 1], ysend.at[1, q], yrecv.at[1, q], device)

        part[q] = product(q, 0)

    def gather(q):
        wait(yrecode.at[q], yrecv.at[0, q])
        wait(yregain.at[q], yrecv.at[1, q])
        total = part[q]
        for d in range(3):
            total += decode(yrecode.at[q, d], yregain.at[q, d])
        part[q] = total

    first, second = pl.ds(0, 256), pl.ds(256, 256)

    def pass_on(m, value, dz):
        encode(value, code.at[m], gain.at[m])
        send(code.at[m], recode.at[m], zsend.at[m], zrecv.at[m], along_z(dz))
        send(gain.at[m], regain.at[m], zsend.at[6 + m], zrecv.at[6 + m], along_z(dz))

    def received(m):
        wait(recode.at[m], zrecv.at[m])
        wait(regain.at[m], zrecv.at[6 + m])
        return decode(recode.at[m], regain.at[m])

    shared[0].wait()
    wait(cbuf.at[0, pl.ds(128, 384)], crecv.at[0])
    scatter(0)
    shared[1].wait()
    wait(cbuf.at[1, pl.ds(128, 384)], crecv.at[1])
    scatter(1)

    shared[2].wait()
    shared[3].wait()
    wait(dpart.at[pl.ds(1, 7)], drecv.at[0])
    total = danchor[...] - dpart[0].astype(jnp.float32)
    for j in range(1, 8):
        total += danchor[...] - dpart[j].astype(jnp.float32)
    dsum[mine] = total / 8

    for j in (2, 4, 6):
        send(dsum.at[mine], dsum.at[mine], dsend.at[1], drecv.at[1], other(j))
    sibling = (rep + 1 - 2 * (rep % 2), row)
    send(dsum.at[mine], dsum.at[mine], dsend.at[2], drecv.at[2], sibling)

    sent(0)
    features(3)
    sent(1)
    features(2)
    gather(0)

    @pl.when(lower < 2)
    def _():
        pl.semaphore_wait(ready.at[1], 2 - lower)

    pass_on(0, part[0, :, first], 1)
    pass_on(1, part[0, :, second], 3)
    gather(1)
    pass_on(2, part[1, :, second], 1)
    scatter(2)
    scatter(3)
    pass_on(4, part[1, :, first] + received(0), 1)
    gather(2)
    pass_on(3, part[2, :, first], 3)
    pass_on(5, part[2, :, second] + received(1), 3)
    wait(dsum.at[pl.ds(0, 48)], drecv.at[1])
    for j in (2, 4, 6):
        there = pl.ds(pl.multiple_of(((rep + j) % 8) * 16, 16), 16)
        send(dsum.at[there], dsum.at[there], dsend.at[3], drecv.at[3], sibling)
    gather(3)

    wait(dsum.at[pl.ds(0, 16)], drecv.at[2])
    wait(dsum.at[pl.ds(0, 48)], drecv.at[3])
    delta[...] = dsum[...]
    part[3, :, second] += received(2)
    part[3, :, first] += received(3)
    grad[:, first] = part[3, :, first] + received(4)
    grad[:, second] = part[3, :, second] + received(5)

    for q in range(4):
        if q > 1:
            sent(q)
        wait(ycode.at[q], ysend.at[0, q])
        wait(ygain.at[q], ysend.at[1, q])
    wait(cbuf.at[0, pl.ds(128, 384)], csend.at[0])
    wait(cbuf.at[1, pl.ds(128, 384)], csend.at[1])
    for m in range(6):
        wait(code.at[m], zsend.at[m])
        wait(gain.at[m], zsend.at[6 + m])
    wait(dpart.at[pl.ds(1, 7)], dsend.at[0])
    wait(dsum.at[pl.ds(0, 48)], dsend.at[1])
    wait(dsum.at[pl.ds(0, 16)], dsend.at[2])
    wait(dsum.at[pl.ds(0, 48)], dsend.at[3])


def update(
    corr_one, corr_two, grad, delta, weight, first, second, anchor, momentum,
    new_weight, new_first, new_second, new_anchor, new_momentum,
):
    slope = grad[...]
    moment = 0.9 * first[0] + 0.1 * slope
    square = 0.999 * second[0] + 0.001 * slope * slope
    new_first[0] = moment
    new_second[0] = square
    step = moment / corr_one[0] / (jnp.sqrt(square / corr_two[0]) + 1e-08)
    new_weight[0] = weight[0] - 0.01 * (step + 0.1 * weight[0])
    change = delta[...]
    speed = 0.9 * momentum[...] + change
    new_momentum[...] = speed
    new_anchor[...] = anchor[...] - 0.7 * (change + 0.9 * speed)


def body(
    hidden,
    key_cotangent,
    key_weight,
    first_moment,
    second_moment,
    step_index,
    anchor,
    outer_momentum,
    replica_fragment,
):
    dma = pltpu.SemaphoreType.DMA
    grad, delta = pl.pallas_call(
        exchange,
        out_shape=[jax.ShapeDtypeStruct((128, 512), jnp.float32)] * 2,
        in_specs=[pl.BlockSpec(memory_space=pl.ANY)] * 4,
        out_specs=[pl.BlockSpec(memory_space=pltpu.VMEM)] * 2,
        scratch_shapes=[
            pltpu.VMEM((4, 512, 512), jnp.bfloat16),
            pltpu.VMEM((2, 512, 512), jnp.bfloat16),
            pltpu.VMEM((4, 3, 128, 512), jnp.int16),
            pltpu.VMEM((4, 3, 4, 128), jnp.float32),
            pltpu.VMEM((4, 3, 128, 512), jnp.int16),
            pltpu.VMEM((4, 3, 4, 128), jnp.float32),
            pltpu.VMEM((4, 128, 512), jnp.float32),
            pltpu.VMEM((6, 128, 256), jnp.int16),
            pltpu.VMEM((6, 2, 128), jnp.float32),
            pltpu.VMEM((6, 128, 256), jnp.int16),
            pltpu.VMEM((6, 2, 128), jnp.float32),
            pltpu.VMEM((8, 16, 512), jnp.bfloat16),
            pltpu.VMEM((16, 512), jnp.float32),
            pltpu.VMEM((128, 512), jnp.float32),
            dma((8,)), dma((4,)), dma((4,)), dma((2,)), dma((2,)), dma((2, 4)), dma((2, 4)),
            dma((12,)), dma((12,)), dma((4,)), dma((4,)), pltpu.SemaphoreType.REGULAR((2,)),
        ],
        compiler_params=pltpu.CompilerParams(
            collective_id=0, has_side_effects=True, vmem_limit_bytes=60 * 1024 * 1024
        ),
        cost_estimate=pl.CostEstimate(flops=2 * 2048 * 512 * 512, bytes_accessed=8 << 20, transcendentals=0),
        name="exchange",
    )(hidden, key_cotangent, replica_fragment, anchor)
    steps = step_index.astype(jnp.float32)
    corr_one = 1.0 - jnp.power(jnp.float32(0.9), steps)
    corr_two = 1.0 - jnp.power(jnp.float32(0.999), steps)
    parts = 2
    scalar = pl.BlockSpec(memory_space=pltpu.SMEM)
    flat = pl.BlockSpec((128 // parts, 512), lambda i: (i, 0))
    deep = pl.BlockSpec((1, 128 // parts, 512), lambda i: (0, i, 0))
    return pl.pallas_call(
        update,
        grid=(parts,),
        out_shape=[jax.ShapeDtypeStruct((1, 128, 512), jnp.float32)] * 3 + [jax.ShapeDtypeStruct((128, 512), jnp.float32)] * 2,
        in_specs=[scalar] * 2 + [flat] * 2 + [deep] * 3 + [flat] * 2,
        out_specs=[deep] * 3 + [flat] * 2,
        name="update",
    )(corr_one[None], corr_two[None], grad, delta, key_weight, first_moment, second_moment, anchor, outer_momentum)


def solution(mesh):
    return jax.shard_map(
        body,
        mesh=mesh,
        in_specs=(
            P(("replica", "fsdp"), None),
            P(("replica", "fsdp"), None),
            P("replica", "fsdp", None),
            P("replica", "fsdp", None),
            P("replica", "fsdp", None),
            P(),
            P("fsdp", None),
            P("fsdp", None),
            P("replica", "fsdp", None),
        ),
        out_specs=(
            P("replica", "fsdp", None),
            P("replica", "fsdp", None),
            P("replica", "fsdp", None),
            P("fsdp", None),
            P("fsdp", None),
        ),
        check_vma=False,
    )
```

time: 67.4 us -> 63.4 us (0.941)
  the two profiles are of different devices: /device:TPU:6 before, /device:TPU:8 now
where the time goes in v3:
time: 63.4 us; the launch traced here: 63.2 us
  Pallas kernels  61.8 us (97%)
  between operations  1.37 us (2%)
    pallas_call x1, Pallas kernels, body(): pl.pallas_call(exchange, out_shape=[jax.ShapeDtypeStruct((128, 512), jnp....  59.4 us
    pallas_call x1, Pallas kernels, body(): pl.pallas_call(update, grid=(parts,), out_shape=[jax.ShapeDtypeStruct((1,...  2.46 us

profile of v3, /device:TPU:8, one launch (start us, length us, event | category | flops | bytes accessed | tf_op | source)
XLA Modules:
  0.0 63.2 jit_solution(654554661495443717)
XLA Ops:
  1.4 59.4 %exchange.1 = (f32[128,512]{1,0:T(8,128)}, f32[128,512]{1,0:T(8,128)}) custom-call(bf16[128,8192]{1,0:T(8,128)(2,1)} %hidden.1, bf16[128,512]{1,0:T(8,128)(2,1)} %cotan.1, bf16[1,128,512]{2,1,0:T(8,128)(2,1)} %frag.1, f32[128,512]{1,0:T(8,128)} %anchor.3), custom_call_target="tpu_custom_call" | custom-call | flops 1073741824 | bytes 8388608 | tf_op jit(solution)/shard_map/exchange/pallas_call | solution.py:267
  60.7 2.5 %update.1 = (f32[1,128,512]{2,1,0:T(8,128)}, f32[1,128,512]{2,1,0:T(8,128)}, f32[1,128,512]{2,1,0:T(8,128)}, f32[128,512]{1,0:T(8,128)}, f32[128,512]{1,0:T(8,128)}) custom-call(f32[1]{0:T(128)} %bitcast.corr_one, f32[1]{0:T(128)} %bitcast.1.corr_two, f32[128,512]{1,0:T(8,128)} %get-tuple-element.7.grad, f32[128,512]{1,0:T(8,128)} %get-tuple-element.8.delta, ...), custom_call_target="tpu_custom_call" | custom-call | tf_op jit(solution)/shard_map/update/pallas_call | solution.py:303

commit v4 on v3

--- a/solution.py
+++ b/solution.py
@@ -9,7 +9,7 @@
 
 MESH = pl.DeviceIdType.MESH
 STEPS = (2, 1, 3, 0)
-BY_X = (True, False, False, True)
+BY_X = (True, False, True, False)
 
 
 def exchange(
@@ -165,6 +165,8 @@
         wait(regain.at[m], zrecv.at[6 + m])
         return decode(recode.at[m], regain.at[m])
 
+    sent(0)
+    features(2)
     shared[0].wait()
     wait(cbuf.at[0, pl.ds(128, 384)], crecv.at[0])
     scatter(0)
@@ -185,10 +187,6 @@
     sibling = (rep + 1 - 2 * (rep % 2), row)
     send(dsum.at[mine], dsum.at[mine], dsend.at[2], drecv.at[2], sibling)
 
-    sent(0)
-    features(3)
-    sent(1)
-    features(2)
     gather(0)
 
     @pl.when(lower < 2)
@@ -200,11 +198,13 @@
     gather(1)
     pass_on(2, part[1, :, second], 1)
     scatter(2)
-    scatter(3)
+    sent(1)
+    features(3)
     pass_on(4, part[1, :, first] + received(0), 1)
     gather(2)
     pass_on(3, part[2, :, first], 3)
     pass_on(5, part[2, :, second] + received(1), 3)
+    scatter(3)
     wait(dsum.at[pl.ds(0, 48)], drecv.at[1])
     for j in (2, 4, 6):
         there = pl.ds(pl.multiple_of(((rep + j) % 8) * 16, 16), 16)

time: 63.4 us -> 62 us (0.978)
  the two profiles are of different devices: /device:TPU:8 before, /device:TPU:6 now
where the time goes in v4:
time: 62 us; the launch traced here: 61.8 us
  Pallas kernels  60.5 us (98%)
  between operations  1.37 us (2%)
    pallas_call x1, Pallas kernels, body(): pl.pallas_call(exchange, out_shape=[jax.ShapeDtypeStruct((128, 512), jnp....  58 us
    pallas_call x1, Pallas kernels, body(): pl.pallas_call(update, grid=(parts,), out_shape=[jax.ShapeDtypeStruct((1,...  2.46 us

profile of v4, /device:TPU:6, one launch (start us, length us, event | category | flops | bytes accessed | tf_op | source)
XLA Modules:
  0.0 61.8 jit_solution(16231119312215492877)
XLA Ops:
  1.4 58.0 %exchange.1 = (f32[128,512]{1,0:T(8,128)}, f32[128,512]{1,0:T(8,128)}) custom-call(bf16[128,8192]{1,0:T(8,128)(2,1)} %hidden.1, bf16[128,512]{1,0:T(8,128)(2,1)} %cotan.1, bf16[1,128,512]{2,1,0:T(8,128)(2,1)} %frag.1, f32[128,512]{1,0:T(8,128)} %anchor.3), custom_call_target="tpu_custom_call" | custom-call | flops 1073741824 | bytes 8388608 | tf_op jit(solution)/shard_map/exchange/pallas_call | solution.py:267
  59.4 2.5 %update.1 = (f32[1,128,512]{2,1,0:T(8,128)}, f32[1,128,512]{2,1,0:T(8,128)}, f32[1,128,512]{2,1,0:T(8,128)}, f32[128,512]{1,0:T(8,128)}, f32[128,512]{1,0:T(8,128)}) custom-call(f32[1]{0:T(128)} %bitcast.corr_one, f32[1]{0:T(128)} %bitcast.1.corr_two, f32[128,512]{1,0:T(8,128)} %get-tuple-element.7.grad, f32[128,512]{1,0:T(8,128)} %get-tuple-element.8.delta, ...), custom_call_target="tpu_custom_call" | custom-call | tf_op jit(solution)/shard_map/update/pallas_call | solution.py:303

commit v5 on v4

--- a/solution.py
+++ b/solution.py
@@ -91,14 +91,14 @@
         def _():
             pl.semaphore_signal(ready.at[1], inc=1, device_id=along_z(dz), device_id_type=MESH)
 
-    for d in (1, 3, 2):
+    for d in (2, 1, 3):
         send(cotan, cbuf.at[0, pl.ds(d * 128, 128)], csend.at[0], crecv.at[0], along_x(d))
         send(cotan, cbuf.at[1, pl.ds(d * 128, 128)], csend.at[1], crecv.at[1], along_y(d))
 
     def features(q):
         @pl.loop(0, 12)
         def _(k):
-            a, b = 1 + k // 4, k % 4
+            a, b = 1 + (k // 4 + 1) % 3, k % 4
             device = along_x(a) if BY_X[q] else along_y(a)
             send(block(q, b, a), place(q, b, a), hsend.at[q], hrecv.at[q], device)
 
@@ -136,8 +136,9 @@
         wait(hbuf.at[q, pl.ds(0, 128)], local.at[q])
         wait(hbuf.at[q, pl.ds(128, 384)], hrecv.at[q])
 
-        @pl.loop(1, 4)
-        def _(b):
+        @pl.loop(0, 3)
+        def _(i):
+            b = 1 + (i + 1) % 3
             encode(product(q, b), ycode.at[q, b - 1], ygain.at[q, b - 1])
             device = along_y(b) if BY_X[q] else along_x(b)
             send(ycode.at[q, b - 1], yrecode.at[q, b - 1], ysend.at[0, q], yrecv.at[0, q], device)

time: 62 us -> 64.4 us (1.039); the launches traced: 61.8 us -> 63.3 us
  Pallas kernels: 60.5 us -> 61.9 us
    pallas_call x1, Pallas kernels: 58 us -> 59.5 us  [body(): pl.pallas_call(exchange, out_shape=[jax.ShapeDtypeStruct((128, 512), jnp....]
where the time goes in v5:
time: 64.4 us; the launch traced here: 63.3 us
  Pallas kernels  61.9 us (96%)
  between operations  1.37 us (2%)
    pallas_call x1, Pallas kernels, body(): pl.pallas_call(exchange, out_shape=[jax.ShapeDtypeStruct((128, 512), jnp....  59.5 us
    pallas_call x1, Pallas kernels, body(): pl.pallas_call(update, grid=(parts,), out_shape=[jax.ShapeDtypeStruct((1,...  2.46 us

profile of v5, /device:TPU:6, one launch (start us, length us, event | category | flops | bytes accessed | tf_op | source)
XLA Modules:
  0.0 63.3 jit_solution(14279316044872021196)
XLA Ops:
  1.4 59.5 %exchange.1 = (f32[128,512]{1,0:T(8,128)}, f32[128,512]{1,0:T(8,128)}) custom-call(bf16[128,8192]{1,0:T(8,128)(2,1)} %hidden.1, bf16[128,512]{1,0:T(8,128)(2,1)} %cotan.1, bf16[1,128,512]{2,1,0:T(8,128)(2,1)} %frag.1, f32[128,512]{1,0:T(8,128)} %anchor.3), custom_call_target="tpu_custom_call" | custom-call | flops 1073741824 | bytes 8388608 | tf_op jit(solution)/shard_map/exchange/pallas_call | solution.py:268
  60.8 2.5 %update.1 = (f32[1,128,512]{2,1,0:T(8,128)}, f32[1,128,512]{2,1,0:T(8,128)}, f32[1,128,512]{2,1,0:T(8,128)}, f32[128,512]{1,0:T(8,128)}, f32[128,512]{1,0:T(8,128)}) custom-call(f32[1]{0:T(128)} %bitcast.corr_one, f32[1]{0:T(128)} %bitcast.1.corr_two, f32[128,512]{1,0:T(8,128)} %get-tuple-element.7.grad, f32[128,512]{1,0:T(8,128)} %get-tuple-element.8.delta, ...), custom_call_target="tpu_custom_call" | custom-call | tf_op jit(solution)/shard_map/update/pallas_call | solution.py:304
